TPU v7x, 128 devices: a whole 4x4x4 slice. The times are simulated.
128 devices in a mesh: row: 16 (over y, x), col: 8 (over z, core).
Axes of the slice: x: 4, y: 4, z: 4, core: 2. Of those that a mesh axis runs over, the one named last changes fastest.
Arguments:
- statistic: float32 [16384, 16384], P('row', 'col'), may hold values from -6 to 6
- noise: bfloat16 [16384, 16384], P('row', 'col'), may hold values from -12 to 12
- grads: bfloat16 [16384, 4096], P('row', 'col'), may hold values from -1.5 to 1.5
Outputs:
- updated: float32 [16384, 16384], P('row', 'col')
All inputs are finite; a program needn't handle non-finite values.
Results may differ from a plain program's by a relative error of at most 0.0003.
Values may be sent and summed in bfloat16 or wider, within the bound.
No kernel may reach another device: no remote copies, remote signals or barrier semaphores. Data moves between devices by JAX's collectives and lax.ppermute only.
A program may use at most 640 MiB of HBM per device.

v0:
```python
import functools

import jax
import jax.numpy as jnp
from jax import lax
from jax.experimental import pallas as pl
from jax.experimental.pallas import tpu as pltpu
from jax.sharding import PartitionSpec as P

AXES = ("row", "col")
SIDE = 4
ORDER = (0, 1, 3, 2)
ROWS_TILE = 512
STREAMS = 2


def place(y, x, z, core):
    return (y % SIDE * SIDE + x % SIDE) * 2 * SIDE + z % SIDE * 2 + core


def coords():
    for y in range(SIDE):
        for x in range(SIDE):
            for z in range(SIDE):
                for core in range(2):
                    yield y, x, z, core


def turn(t):
    return t if t % 2 else (t + 2) % SIDE


def spread_pairs():
    pairs = []
    for y, x, z, core in coords():
        half = x // 2
        to_x = x if core == half else SIDE - 1 - x
        pairs.append((place(y, x, z, core), place(y + turn((z - y) % SIDE), to_x, y, half)))
    return pairs


def shift_pairs(step, first):
    pairs = []
    for y, x, z, core in coords():
        along_x = (core == 0) == first
        to = place(y, x - step, z, core) if along_x else place(y - step, x, z, core)
        pairs.append((place(y, x, z, core), to))
    return pairs


def unit_ids(offsets):
    row, col = lax.axis_index("row"), lax.axis_index("col")
    y, x, z, core = row // SIDE, row % SIDE, col // 2, col % 2
    blocks, eighths = [], []
    for j in offsets:
        for i in ORDER:
            uy = (y + jnp.where(core == 0, j, i)) % SIDE
            ux = (x + jnp.where(core == 0, i, j)) % SIDE
            t = (uy - z) % SIDE
            k = (z + jnp.where(t % 2 == 1, t, (t + 2) % SIDE)) % SIDE
            home = ux // 2 == core
            source_x = jnp.where(home, ux, SIDE - 1 - ux)
            blocks.append(source_x % 2)
            eighths.append(2 * k + jnp.where(home, core, 1 - core))
    return blocks, eighths, [row, col]


def tables(held):
    blocks, eighths, place_ids = held
    ones = sum(blocks)
    zeros = len(blocks) - ones
    slots, seen = [], jnp.int32(0)
    for n, block in enumerate(blocks):
        slots.append(jnp.where(block == 1, zeros + seen, n - seen))
        seen = seen + block
    return jnp.stack(slots + eighths + [zeros] + place_ids).astype(jnp.int32)


def blend_kernel(streams, pieces, fresh, table, panel, *refs):
    count = 1 + max(g for units in pieces for g, _ in units)
    groups, refs = refs[:count], refs[count:]
    carried, refs = refs[: 2 if fresh else 1], refs[2 if fresh else 1 :]
    out, left, right, tiles, added, lookup, left_sems, right_sems, in_sems, out_sems = refs[-10:]
    sources = [[groups[g].at[s] for g, s in units] for units in pieces]
    n = len(sources[0])
    eighths, rows, depth = left.shape
    width = right.shape[1]
    tile = tiles.shape[1]
    steps = [(m, q, b) for m in range(rows // tile) for q in range(len(streams)) for b in range(2)]

    def copy_right(q, u):
        slot = q * n + table[u]
        return pltpu.make_async_copy(sources[q][u], right.at[slot], right_sems.at[slot])

    def copy_left(s, m):
        eighth, span = s if fresh else table[n + s], pl.ds(m * tile, tile)
        return pltpu.make_async_copy(panel.at[eighth, span], left.at[s, span], left_sems.at[m, s])

    def window(ref, m, q, b):
        return ref.at[pl.ds(m * tile, tile), pl.ds((STREAMS * b + streams[q]) * width, width)]

    def copies_in(t):
        copies = [pltpu.make_async_copy(window(carried[0], *steps[t]), tiles.at[t], in_sems.at[0, t])]
        if fresh:
            copies.append(pltpu.make_async_copy(window(carried[1], *steps[t]), added.at[t], in_sems.at[1, t]))
        return copies

    def copy_out(t):
        return pltpu.make_async_copy(tiles.at[t], window(out, *steps[t]), out_sems.at[t])

    for s in range(eighths):
        copy_left(s, 0).start()
    for copy in copies_in(0):
        copy.start()
    for q in range(len(streams)):
        for u in range(n):
            copy_right(q, u).start()
    for t in range(1, len(steps)):
        if not fresh and steps[t][1:] == (0, 0):
            for s in range(eighths):
                copy_left(s, steps[t][0]).start()
        for copy in copies_in(t):
            copy.start()
    for u in range(n):
        lookup[table[u]] = table[n + u] if fresh else u

    zeros = table[2 * n]
    for t, (m, q, b) in enumerate(steps):
        first = q == 0 and b == 0
        if first:
            for s in range(eighths):
                copy_left(s, m).wait()
        for copy in copies_in(t):
            copy.wait()
        if fresh and first and m + 1 < rows // tile:
            for s in range(eighths):
                copy_left(s, m + 1).start()
        if fresh:
            tiles[t] = 0.9 * tiles[t] + 0.1 * added[t].astype(jnp.float32)

        def pair(p, _):
            if m == 0:
                for s in range(2):
                    slot = q * n + 2 * p + s
                    pltpu.make_async_copy(sources[0][0], right.at[slot], right_sems.at[slot]).wait()
            parts = [
                lax.dot_general(
                    left[lookup[2 * p + s], m * tile : (m + 1) * tile, :],
                    right[q * n + 2 * p + s],
                    (((1,), (1,)), ((), ())),
                    preferred_element_type=jnp.float32,
                )
                for s in range(2)
            ]
            tiles[t] += 0.1 * (parts[0] + parts[1])
            return 0

        lax.fori_loop(0 if b == 0 else zeros // 2, zeros // 2 if b == 0 else n // 2, pair, 0)
        at_row = table[2 * n + 1] * rows + m * tile + lax.broadcasted_iota(jnp.int32, (tile, width), 0)
        at_col = (table[2 * n + 2] * 2 + b) * (width * STREAMS) + streams[q] * width
        at_col = at_col + lax.broadcasted_iota(jnp.int32, (tile, width), 1)
        tiles[t] = jnp.where(at_row >= at_col, tiles[t], 0.0)
        copy_out(t).start()
    for t in range(len(steps)):
        copy_out(t).wait()


def blend(streams, pieces, table, panel, groups, fresh, before):
    eighths, rows, depth = panel.shape
    n, width = len(pieces[0]), groups[0].shape[1]
    held = n if fresh is None else eighths
    count = 2 * len(streams) * rows // ROWS_TILE
    carried = [before] if fresh is None else list(fresh)
    extra = [] if fresh is None or before is None else [before]
    operands = [table, panel, *groups, *carried, *extra]
    anywhere = pl.BlockSpec(memory_space=pl.ANY)
    return pl.pallas_call(
        functools.partial(blend_kernel, streams, pieces, fresh is not None),
        in_specs=[pl.BlockSpec(memory_space=pltpu.SMEM)] + [anywhere] * (len(operands) - 1),
        out_specs=anywhere,
        scratch_shapes=[
            pltpu.VMEM((held, rows, depth), jnp.bfloat16),
            pltpu.VMEM((len(streams) * n, width, depth), jnp.bfloat16),
            pltpu.VMEM((count, ROWS_TILE, width), jnp.float32),
            pltpu.VMEM((count if fresh else 1, ROWS_TILE, width), jnp.bfloat16),
            pltpu.SMEM((n,), jnp.int32),
            pltpu.SemaphoreType.DMA((rows // ROWS_TILE, held)),
            pltpu.SemaphoreType.DMA((len(streams) * n,)),
            pltpu.SemaphoreType.DMA((2, count)),
            pltpu.SemaphoreType.DMA((count,)),
        ],
        out_shape=jax.ShapeDtypeStruct((rows, 2 * STREAMS * width), jnp.float32),
        input_output_aliases={} if before is None else {len(operands) - 1: 0},
        compiler_params=pltpu.CompilerParams(vmem_limit_bytes=58 * 2**20),
        cost_estimate=pl.CostEstimate(
            flops=2 * len(streams) * n * rows * width * depth, bytes_accessed=24 * 2**20, transcendentals=0
        ),
    )(*operands)


def move(array, pairs):
    return lax.ppermute(array, AXES, pairs)


def shards(statistic, noise, grads):
    part = grads.shape[0] // STREAMS
    first = move(grads[:part], spread_pairs())
    first, rest = lax.optimization_barrier((first, grads))
    panel = lax.all_gather(rest, "col", axis=0)
    heads = [first, move(rest[part:], spread_pairs())]
    near, far = tables(unit_ids((0, 1, 3))), tables(unit_ids((2,)))
    inputs = (statistic, noise)

    def gather(unit):
        own = jnp.stack([unit] + [move(unit, shift_pairs(i, True)) for i in (1, -1, 2)])
        return own, move(own, shift_pairs(1, False)), move(own, shift_pairs(-1, False))

    def forward(ahead, behind):
        return move(ahead[:2], shift_pairs(1, False)), move(behind[2:], shift_pairs(-1, False))

    held = [gather(unit) for unit in heads]
    units = [tuple((g, s) for g in range(3) for s in range(SIDE))]
    distant = forward(*held[0][1:])
    total = blend((0,), units, near, panel, held[0], inputs, None)
    (own, ahead, behind), total = lax.optimization_barrier((held[1], total))
    distant += forward(ahead, behind)
    total = blend((1,), units, near, panel, (own, ahead, behind), inputs, total)
    units = [tuple((2 * q + g, s) for g in range(2) for s in range(2)) for q in range(STREAMS)]
    return blend((0, 1), units, far, panel, distant, None, total)


def solution(mesh):
    in_specs = (P("row", "col"), P("row", "col"), P("row", "col"))
    out_specs = P("row", "col")
    return jax.shard_map(shards, mesh=mesh, in_specs=in_specs, out_specs=out_specs, check_vma=False)
```

profile of v0, /device:TPU:25, one launch (start us, length us, event | category | flops | bytes accessed | tf_op | source)
XLA Modules:
  0.0 164.4 jit_solution(3757436584791049693)
XLA Ops:
  6.5 0.0 copy-start.1
  6.5 0.0 all-gather.3.cloned.1.call-start
  6.5 1.2 slice.18
  7.7 6.2 %collective-permute-start = (bf16[512,512]{1,0:T(8,128)(2,1)S(1)}, bf16[512,512]{1,0:T(8,128)(2,1)S(1)}, u32[]{:S(2)}, u32[]{:S(2)}) collective-permute-start(bf16[512,512]{1,0:T(8,128)(2,1)S(1)} %slice.18), channel_id=1, source_target_pairs={{0,64},{1,88},{2,32},{3,56},{4,0},{5,24},{6,96},{7,120},{8,72},{9,... | collective-permute-start | bytes 1572872 | tf_op jit(solution)/shard_map/ppermute | solution.py:202
  13.9 8.0 %collective-permute-done = bf16[512,512]{1,0:T(8,128)(2,1)S(1)} collective-permute-done((bf16[512,512]{1,0:T(8,128)(2,1)S(1)}, bf16[512,512]{1,0:T(8,128)(2,1)S(1)}, u32[]{:S(2)}, u32[]{:S(2)}) %collective-permute-start) | collective-permute-done | bytes 524320 | tf_op jit(solution)/shard_map/ppermute | solution.py:202
  21.9 0.0 all-gather.3.cloned.1.call-update
  21.9 0.0 copy-done.1
  22.0 6.2 %collective-permute-start.8 = (bf16[512,512]{1,0:T(8,128)(2,1)S(1)}, bf16[512,512]{1,0:T(8,128)(2,1)S(1)}, u32[]{:S(2)}, u32[]{:S(2)}) collective-permute-start(bf16[512,512]{1,0:T(8,128)(2,1)S(1)} %slice.21), channel_id=1, source_target_pairs={{0,64},{1,88},{2,32},{3,56},{4,0},{5,24},{6,96},{7,120},{8,72},{9,... | collective-permute-start | bytes 1572872 | tf_op jit(solution)/shard_map/ppermute | solution.py:202
  28.2 0.0 collective-permute-start.3
  28.2 1.2 collective-permute-start.2
  29.4 0.2 collective-permute-start.1
  29.7 13.6 %collective-permute-done.8 = bf16[512,512]{1,0:T(8,128)(2,1)S(1)} collective-permute-done((bf16[512,512]{1,0:T(8,128)(2,1)S(1)}, bf16[512,512]{1,0:T(8,128)(2,1)S(1)}, u32[]{:S(2)}, u32[]{:S(2)}) %collective-permute-start.8) | collective-permute-done | bytes 524320 | tf_op jit(solution)/shard_map/ppermute | solution.py:202
  43.3 0.0 collective-permute-start.11
  43.3 0.1 collective-permute-start.10
  43.4 0.0 collective-permute-done.3
  43.4 1.3 collective-permute-start.9
  44.8 10.5 %collective-permute-done.2 = bf16[512,512]{1,0:T(8,128)(2,1)S(1)} collective-permute-done((bf16[512,512]{1,0:T(8,128)(2,1)S(1)}, bf16[512,512]{1,0:T(8,128)(2,1)S(1)}, u32[]{:S(2)}, u32[]{:S(2)}) %collective-permute-start.2) | collective-permute-done | bytes 524320 | tf_op jit(solution)/shard_map/ppermute | solution.py:202
  55.3 0.0 collective-permute-done.1
  55.3 1.6 pad_maximum_fusion.refs_0_
  56.9 0.0 collective-permute-start.6
  56.9 2.7 %collective-permute-start.4 = (bf16[4,512,512]{2,1,0:T(8,128)(2,1)}, bf16[4,512,512]{2,1,0:T(8,128)(2,1)}, u32[]{:S(2)}, u32[]{:S(2)}) collective-permute-start(bf16[4,512,512]{2,1,0:T(8,128)(2,1)} %pad_maximum_fusion.refs_0_), channel_id=1, source_target_pairs={{0,96},{1,25},{2,98},{3,27},{4,100},{5,29},{6,102},{7,31},{8,104},... | collective-permute-start | bytes 6291464 | tf_op jit(solution)/shard_map/ppermute | solution.py:202
  59.5 0.0 collective-permute-done.11
  59.5 1.4 collective-permute-done.10
  61.0 0.0 collective-permute-done.9
  61.0 0.3 pad_maximum_fusion.1.refs_0_
  61.3 0.0 copy-start
  61.3 0.1 collective-permute-start.13
  61.4 11.3 %collective-permute-start.12 = (bf16[4,512,512]{2,1,0:T(8,128)(2,1)S(1)}, bf16[4,512,512]{2,1,0:T(8,128)(2,1)}, u32[]{:S(2)}, u32[]{:S(2)}) collective-permute-start(bf16[4,512,512]{2,1,0:T(8,128)(2,1)S(1)} %pad_maximum_fusion.1.refs_0_), channel_id=1, source_target_pairs={{0,96},{1,25},{2,98},{3,27},{4,100},{5,29},{6,102},{7,31},{8,104},... | collective-permute-start | bytes 6291464 | tf_op jit(solution)/shard_map/ppermute | solution.py:202
  72.6 0.7 stack.193.table
  73.3 21.5 %collective-permute-done.6.refs_2_ = bf16[4,512,512]{2,1,0:T(8,128)(2,1)} collective-permute-done((bf16[4,512,512]{2,1,0:T(8,128)(2,1)}, bf16[4,512,512]{2,1,0:T(8,128)(2,1)}, u32[]{:S(2)}, u32[]{:S(2)}) %collective-permute-start.6) | collective-permute-done | bytes 2097184 | tf_op jit(solution)/shard_map/ppermute | solution.py:202
  94.8 2.3 %slice.25 = bf16[2,512,512]{2,1,0:T(8,128)(2,1)} slice(bf16[4,512,512]{2,1,0:T(8,128)(2,1)} %collective-permute-done.6.refs_2_), slice={[2:4], [0:512], [0:512]} | slice | bytes 2097152 | tf_op jit(solution)/shard_map/slice | solution.py:219
  97.1 0.0 copy-done
  97.1 0.0 collective-permute-start.7
  97.1 0.0 collective-permute-done.4.refs_1_
  97.1 2.3 %slice.24 = bf16[2,512,512]{2,1,0:T(8,128)(2,1)} slice(bf16[4,512,512]{2,1,0:T(8,128)(2,1)} %collective-permute-done.4.refs_1_), slice={[0:2], [0:512], [0:512]} | slice | bytes 2097152 | tf_op jit(solution)/shard_map/slice | solution.py:219
  99.4 2.7 %collective-permute-start.5 = (bf16[2,512,512]{2,1,0:T(8,128)(2,1)}, bf16[2,512,512]{2,1,0:T(8,128)(2,1)}, u32[]{:S(2)}, u32[]{:S(2)}) collective-permute-start(bf16[2,512,512]{2,1,0:T(8,128)(2,1)} %slice.24), channel_id=1, source_target_pairs={{0,96},{1,25},{2,98},{3,27},{4,100},{5,29},{6,102},{7,31},{8,104},... | collective-permute-start | bytes 3145736 | tf_op jit(solution)/shard_map/ppermute | solution.py:202
  102.0 0.0 all-gather.3.cloned.1.call-done
  102.0 17.4 %shard_map.37.refs_5_ = f32[1024,2048]{1,0:T(8,128)} custom-call(s32[27]{0:T(128)} %stack.193.table, bf16[8,1024,512]{2,1,0:T(8,128)(2,1)} %bitcast.45, bf16[4,512,512]{2,1,0:T(8,128)(2,1)} %pad_maximum_fusion.refs_0_, bf16[4,512,512]{2,1,0:T(8,128)(2,1)} %collective-permute-done.4.refs_1_, bf16[4,512,512]{2,1,0:T(8,128)(2,1)} %collective-permute-done.6.refs_2_, ...), custom_call_target="tpu_custom_call" | custom-call | flops 6442450944 | bytes 25165824 | tf_op jit(solution)/shard_map/pallas_call | solution.py:177
  119.4 0.0 collective-permute-done.13.refs_2_
  119.4 0.0 collective-permute-done.12.refs_1_
  119.4 2.3 %slice.23 = bf16[2,512,512]{2,1,0:T(8,128)(2,1)} slice(bf16[4,512,512]{2,1,0:T(8,128)(2,1)} %collective-permute-done.13.refs_2_), slice={[2:4], [0:512], [0:512]} | slice | bytes 2097152 | tf_op jit(solution)/shard_map/slice | solution.py:219
  121.7 2.3 %slice.22 = bf16[2,512,512]{2,1,0:T(8,128)(2,1)} slice(bf16[4,512,512]{2,1,0:T(8,128)(2,1)} %collective-permute-done.12.refs_1_), slice={[0:2], [0:512], [0:512]} | slice | bytes 2097152 | tf_op jit(solution)/shard_map/slice | solution.py:219
  124.0 0.2 collective-permute-start.14
  124.2 1.2 collective-permute-start.15
  125.4 0.7 stack.157.table
  126.1 17.3 %shard_map.38.refs_4_ = f32[1024,2048]{1,0:T(8,128)} custom-call(s32[27]{0:T(128)} %stack.193.table, bf16[8,1024,512]{2,1,0:T(8,128)(2,1)} %bitcast.46, bf16[4,512,512]{2,1,0:T(8,128)(2,1)} %copy-done, bf16[4,512,512]{2,1,0:T(8,128)(2,1)} %collective-permute-done.12.refs_1_, ...), custom_call_target="tpu_custom_call", output_to_operand_aliasing={{}: (7, {})} | custom-call | flops 6442450944 | bytes 25165824 | tf_op jit(solution)/shard_map/pallas_call | solution.py:177
  143.5 0.0 collective-permute-done.7.refs_1_
  143.5 0.0 copy-start.2
  143.5 0.0 collective-permute-done.5.refs_0_
  143.5 0.0 collective-permute-done.14.refs_2_
  143.5 0.0 copy-start.3
  143.5 0.0 collective-permute-done.15.refs_3_
  143.5 0.9 copy-done.2
  144.5 0.3 copy-done.3
  144.8 0.0 copy-start.4
  144.8 1.0 copy-done.4
  145.7 11.8 %shard_map.39 = f32[1024,2048]{1,0:T(8,128)} custom-call(s32[11]{0:T(128)} %stack.157.table, bf16[8,1024,512]{2,1,0:T(8,128)(2,1)} %bitcast.47, bf16[2,512,512]{2,1,0:T(8,128)(2,1)} %collective-permute-done.5.refs_0_, bf16[2,512,512]{2,1,0:T(8,128)(2,1)} %copy-done.2, bf16[2,512,512]{2,1,0:T(8,128)(2,1)} %copy-done.3, ...), custom_call_target="tpu_custom_call", output_to_operand_aliasing={{}: (6, {})} | custom-call | flops 4294967296 | bytes 25165824 | tf_op jit(solution)/shard_map/pallas_call | solution.py:177
  (1 shorter events, 0.0 us)
Async XLA Ops:
  6.5 15.4 %copy-start.1 = (bf16[1024,512]{1,0:T(8,128)(2,1)S(1)}, bf16[1024,512]{1,0:T(8,128)(2,1)}, u32[]{:S(2)}) copy-start(bf16[1024,512]{1,0:T(8,128)(2,1)} %param.5) | copy-start | bytes 3145732
  6.5 95.5 %all-gather.3.cloned.1.call-start = ((), (), s32[]{:S(2)}) async-start(), calls=%async_computation | async-start | bytes 9437184 | tf_op jit(solution)/shard_map/all_gather | solution.py:209
  7.7 14.2 %collective-permute-start = (bf16[512,512]{1,0:T(8,128)(2,1)S(1)}, bf16[512,512]{1,0:T(8,128)(2,1)S(1)}, u32[]{:S(2)}, u32[]{:S(2)}) collective-permute-start(bf16[512,512]{1,0:T(8,128)(2,1)S(1)} %slice.18), channel_id=1, source_target_pairs={{0,64},{1,88},{2,32},{3,56},{4,0},{5,24},{6,96},{7,120},{8,72},{9,... | collective-permute-start | bytes 1572872 | tf_op jit(solution)/shard_map/ppermute | solution.py:202
  22.0 21.3 %collective-permute-start.8 = (bf16[512,512]{1,0:T(8,128)(2,1)S(1)}, bf16[512,512]{1,0:T(8,128)(2,1)S(1)}, u32[]{:S(2)}, u32[]{:S(2)}) collective-permute-start(bf16[512,512]{1,0:T(8,128)(2,1)S(1)} %slice.21), channel_id=1, source_target_pairs={{0,64},{1,88},{2,32},{3,56},{4,0},{5,24},{6,96},{7,120},{8,72},{9,... | collective-permute-start | bytes 1572872 | tf_op jit(solution)/shard_map/ppermute | solution.py:202
  28.2 15.2 %collective-permute-start.3 = (bf16[512,512]{1,0:T(8,128)(2,1)S(1)}, bf16[512,512]{1,0:T(8,128)(2,1)S(1)}, u32[]{:S(2)}, u32[]{:S(2)}) collective-permute-start(bf16[512,512]{1,0:T(8,128)(2,1)S(1)} %collective-permute-done), channel_id=1, source_target_pairs={{0,16},{1,65},{2,18},{3,67},{4,20},{5,69},{6,22},{7,71},{8,24},{9,... | collective-permute-start | bytes 1572872 | tf_op jit(solution)/shard_map/ppermute | solution.py:202
  28.2 27.0 %collective-permute-start.2 = (bf16[512,512]{1,0:T(8,128)(2,1)S(1)}, bf16[512,512]{1,0:T(8,128)(2,1)S(1)}, u32[]{:S(2)}, u32[]{:S(2)}) collective-permute-start(bf16[512,512]{1,0:T(8,128)(2,1)S(1)} %collective-permute-done), channel_id=1, source_target_pairs={{0,8},{1,33},{2,10},{3,35},{4,12},{5,37},{6,14},{7,39},{8,16},{9,4... | collective-permute-start | bytes 1572872 | tf_op jit(solution)/shard_map/ppermute | solution.py:202
  29.4 25.8 %collective-permute-start.1 = (bf16[512,512]{1,0:T(8,128)(2,1)S(1)}, bf16[512,512]{1,0:T(8,128)(2,1)S(1)}, u32[]{:S(2)}, u32[]{:S(2)}) collective-permute-start(bf16[512,512]{1,0:T(8,128)(2,1)S(1)} %collective-permute-done), channel_id=1, source_target_pairs={{0,24},{1,97},{2,26},{3,99},{4,28},{5,101},{6,30},{7,103},{8,0},{9... | collective-permute-start | bytes 1572872 | tf_op jit(solution)/shard_map/ppermute | solution.py:202
  43.3 16.2 %collective-permute-start.11 = (bf16[512,512]{1,0:T(8,128)(2,1)S(1)}, bf16[512,512]{1,0:T(8,128)(2,1)S(1)}, u32[]{:S(2)}, u32[]{:S(2)}) collective-permute-start(bf16[512,512]{1,0:T(8,128)(2,1)S(1)} %collective-permute-done.8), channel_id=1, source_target_pairs={{0,16},{1,65},{2,18},{3,67},{4,20},{5,69},{6,22},{7,71},{8,24},{9,... | collective-permute-start | bytes 1572872 | tf_op jit(solution)/shard_map/ppermute | solution.py:202
  43.3 17.7 %collective-permute-start.10 = (bf16[512,512]{1,0:T(8,128)(2,1)S(1)}, bf16[512,512]{1,0:T(8,128)(2,1)S(1)}, u32[]{:S(2)}, u32[]{:S(2)}) collective-permute-start(bf16[512,512]{1,0:T(8,128)(2,1)S(1)} %collective-permute-done.8), channel_id=1, source_target_pairs={{0,8},{1,33},{2,10},{3,35},{4,12},{5,37},{6,14},{7,39},{8,16},{9,4... | collective-permute-start | bytes 1572872 | tf_op jit(solution)/shard_map/ppermute | solution.py:202
  43.4 17.6 %collective-permute-start.9 = (bf16[512,512]{1,0:T(8,128)(2,1)S(1)}, bf16[512,512]{1,0:T(8,128)(2,1)S(1)}, u32[]{:S(2)}, u32[]{:S(2)}) collective-permute-start(bf16[512,512]{1,0:T(8,128)(2,1)S(1)} %collective-permute-done.8), channel_id=1, source_target_pairs={{0,24},{1,97},{2,26},{3,99},{4,28},{5,101},{6,30},{7,103},{8,0},{9... | collective-permute-start | bytes 1572872 | tf_op jit(solution)/shard_map/ppermute | solution.py:202
  56.9 37.9 %collective-permute-start.6 = (bf16[4,512,512]{2,1,0:T(8,128)(2,1)}, bf16[4,512,512]{2,1,0:T(8,128)(2,1)}, u32[]{:S(2)}, u32[]{:S(2)}) collective-permute-start(bf16[4,512,512]{2,1,0:T(8,128)(2,1)} %pad_maximum_fusion.refs_0_), channel_id=1, source_target_pairs={{0,32},{1,9},{2,34},{3,11},{4,36},{5,13},{6,38},{7,15},{8,40},{9,1... | collective-permute-start | bytes 6291464 | tf_op jit(solution)/shard_map/ppermute | solution.py:202
  56.9 40.2 %collective-permute-start.4 = (bf16[4,512,512]{2,1,0:T(8,128)(2,1)}, bf16[4,512,512]{2,1,0:T(8,128)(2,1)}, u32[]{:S(2)}, u32[]{:S(2)}) collective-permute-start(bf16[4,512,512]{2,1,0:T(8,128)(2,1)} %pad_maximum_fusion.refs_0_), channel_id=1, source_target_pairs={{0,96},{1,25},{2,98},{3,27},{4,100},{5,29},{6,102},{7,31},{8,104},... | collective-permute-start | bytes 6291464 | tf_op jit(solution)/shard_map/ppermute | solution.py:202
  61.3 35.8 %copy-start = (bf16[4,512,512]{2,1,0:T(8,128)(2,1)}, bf16[4,512,512]{2,1,0:T(8,128)(2,1)S(1)}, u32[]{:S(2)}) copy-start(bf16[4,512,512]{2,1,0:T(8,128)(2,1)S(1)} %pad_maximum_fusion.1.refs_0_) | copy-start | bytes 6291460
  61.3 58.1 %collective-permute-start.13 = (bf16[4,512,512]{2,1,0:T(8,128)(2,1)S(1)}, bf16[4,512,512]{2,1,0:T(8,128)(2,1)}, u32[]{:S(2)}, u32[]{:S(2)}) collective-permute-start(bf16[4,512,512]{2,1,0:T(8,128)(2,1)S(1)} %pad_maximum_fusion.1.refs_0_), channel_id=1, source_target_pairs={{0,32},{1,9},{2,34},{3,11},{4,36},{5,13},{6,38},{7,15},{8,40},{9,1... | collective-permute-start | bytes 6291464 | tf_op jit(solution)/shard_map/ppermute | solution.py:202
  61.4 58.1 %collective-permute-start.12 = (bf16[4,512,512]{2,1,0:T(8,128)(2,1)S(1)}, bf16[4,512,512]{2,1,0:T(8,128)(2,1)}, u32[]{:S(2)}, u32[]{:S(2)}) collective-permute-start(bf16[4,512,512]{2,1,0:T(8,128)(2,1)S(1)} %pad_maximum_fusion.1.refs_0_), channel_id=1, source_target_pairs={{0,96},{1,25},{2,98},{3,27},{4,100},{5,29},{6,102},{7,31},{8,104},... | collective-permute-start | bytes 6291464 | tf_op jit(solution)/shard_map/ppermute | solution.py:202
  97.1 46.4 %collective-permute-start.7 = (bf16[2,512,512]{2,1,0:T(8,128)(2,1)}, bf16[2,512,512]{2,1,0:T(8,128)(2,1)S(1)}, u32[]{:S(2)}, u32[]{:S(2)}) collective-permute-start(bf16[2,512,512]{2,1,0:T(8,128)(2,1)} %slice.25), channel_id=1, source_target_pairs={{0,32},{1,9},{2,34},{3,11},{4,36},{5,13},{6,38},{7,15},{8,40},{9,1... | collective-permute-start | bytes 3145736 | tf_op jit(solution)/shard_map/ppermute | solution.py:202
  99.4 44.1 %collective-permute-start.5 = (bf16[2,512,512]{2,1,0:T(8,128)(2,1)}, bf16[2,512,512]{2,1,0:T(8,128)(2,1)}, u32[]{:S(2)}, u32[]{:S(2)}) collective-permute-start(bf16[2,512,512]{2,1,0:T(8,128)(2,1)} %slice.24), channel_id=1, source_target_pairs={{0,96},{1,25},{2,98},{3,27},{4,100},{5,29},{6,102},{7,31},{8,104},... | collective-permute-start | bytes 3145736 | tf_op jit(solution)/shard_map/ppermute | solution.py:202
  124.0 19.5 %collective-permute-start.14 = (bf16[2,512,512]{2,1,0:T(8,128)(2,1)}, bf16[2,512,512]{2,1,0:T(8,128)(2,1)S(1)}, u32[]{:S(2)}, u32[]{:S(2)}) collective-permute-start(bf16[2,512,512]{2,1,0:T(8,128)(2,1)} %slice.22), channel_id=1, source_target_pairs={{0,96},{1,25},{2,98},{3,27},{4,100},{5,29},{6,102},{7,31},{8,104},... | collective-permute-start | bytes 3145736 | tf_op jit(solution)/shard_map/ppermute | solution.py:202
  124.2 19.3 %collective-permute-start.15 = (bf16[2,512,512]{2,1,0:T(8,128)(2,1)}, bf16[2,512,512]{2,1,0:T(8,128)(2,1)S(1)}, u32[]{:S(2)}, u32[]{:S(2)}) collective-permute-start(bf16[2,512,512]{2,1,0:T(8,128)(2,1)} %slice.23), channel_id=1, source_target_pairs={{0,32},{1,9},{2,34},{3,11},{4,36},{5,13},{6,38},{7,15},{8,40},{9,1... | collective-permute-start | bytes 3145736 | tf_op jit(solution)/shard_map/ppermute | solution.py:202
  143.5 1.0 copy-start.2
  143.5 1.3 copy-start.3
  144.8 1.0 copy-start.4
Sparse Core Ops, SparseCore 0:
  22.1 65.3 all-gather.2
where the time goes:
time: 165 us; the launch traced here: 164 us
  waiting for transfers between devices  55.1 us (33%)
  Pallas kernels  46.5 us (28%)
  starting transfers between devices  33.6 us (20%)
  local copies, waits for them, and re-layouts  13.9 us (8%)
  between operations  13.5 us (8%)
  other arithmetic  1.85 us (1%)
    ppermute x16, waiting for transfers between devices, move(): return lax.ppermute(array, AXES, pairs)  55.1 us
    pallas_call x3, Pallas kernels, blend(): pl.pallas_call(functools.partial(blend_kernel, streams, pieces, fresh is...  46.5 us
    ppermute x16, starting transfers between devices, move(): return lax.ppermute(array, AXES, pairs)  33.6 us
    slice x2, local copies, waits for them, and re-layouts, forward(): behind[2:]  4.55 us
    slice x2, local copies, waits for them, and re-layouts, forward(): ahead[:2]  4.53 us
  transfers between devices with their start and end apart: 17, of which 5 were waited for; matrix products, arithmetic and copies ran while one was open for 8% of the time, Pallas kernels for 21%

commit v1 on v0

--- a/solution.py
+++ b/solution.py
@@ -110,17 +110,13 @@
 
     for s in range(eighths):
         copy_left(s, 0).start()
-    for copy in copies_in(0):
-        copy.start()
+    lead = 1 if fresh else 3
+    for t in range(lead):
+        for copy in copies_in(t):
+            copy.start()
     for q in range(len(streams)):
         for u in range(n):
             copy_right(q, u).start()
-    for t in range(1, len(steps)):
-        if not fresh and steps[t][1:] == (0, 0):
-            for s in range(eighths):
-                copy_left(s, steps[t][0]).start()
-        for copy in copies_in(t):
-            copy.start()
     for u in range(n):
         lookup[table[u]] = table[n + u] if fresh else u
 
@@ -132,9 +128,12 @@
                 copy_left(s, m).wait()
         for copy in copies_in(t):
             copy.wait()
-        if fresh and first and m + 1 < rows // tile:
+        if first and m + 1 < rows // tile:
             for s in range(eighths):
                 copy_left(s, m + 1).start()
+        if t + lead < len(steps):
+            for copy in copies_in(t + lead):
+                copy.start()
         if fresh:
             tiles[t] = 0.9 * tiles[t] + 0.1 * added[t].astype(jnp.float32)
 
@@ -156,10 +155,15 @@
             return 0
 
         lax.fori_loop(0 if b == 0 else zeros // 2, zeros // 2 if b == 0 else n // 2, pair, 0)
-        at_row = table[2 * n + 1] * rows + m * tile + lax.broadcasted_iota(jnp.int32, (tile, width), 0)
-        at_col = (table[2 * n + 2] * 2 + b) * (width * STREAMS) + streams[q] * width
-        at_col = at_col + lax.broadcasted_iota(jnp.int32, (tile, width), 1)
-        tiles[t] = jnp.where(at_row >= at_col, tiles[t], 0.0)
+        top = table[2 * n + 1] * rows + m * tile
+        side = (table[2 * n + 2] * 2 + b) * (width * STREAMS) + streams[q] * width
+
+        @pl.when(top < side + width - 1)
+        def _():
+            at_row = top + lax.broadcasted_iota(jnp.int32, (tile, width), 0)
+            at_col = side + lax.broadcasted_iota(jnp.int32, (tile, width), 1)
+            tiles[t] = jnp.where(at_row >= at_col, tiles[t], 0.0)
+
         copy_out(t).start()
     for t in range(len(steps)):
         copy_out(t).wait()
@@ -215,17 +219,14 @@
         own = jnp.stack([unit] + [move(unit, shift_pairs(i, True)) for i in (1, -1, 2)])
         return own, move(own, shift_pairs(1, False)), move(own, shift_pairs(-1, False))
 
-    def forward(ahead, behind):
-        return move(ahead[:2], shift_pairs(1, False)), move(behind[2:], shift_pairs(-1, False))
-
     held = [gather(unit) for unit in heads]
     units = [tuple((g, s) for g in range(3) for s in range(SIDE))]
-    distant = forward(*held[0][1:])
+    distant = [move(held[0][1], shift_pairs(1, False))]
     total = blend((0,), units, near, panel, held[0], inputs, None)
     (own, ahead, behind), total = lax.optimization_barrier((held[1], total))
-    distant += forward(ahead, behind)
+    distant += [move(ahead[:2], shift_pairs(1, False)), move(behind[2:], shift_pairs(-1, False))]
     total = blend((1,), units, near, panel, (own, ahead, behind), inputs, total)
-    units = [tuple((2 * q + g, s) for g in range(2) for s in range(2)) for q in range(STREAMS)]
+    units = [tuple((0, s) for s in range(SIDE)), tuple((1 + g, s) for g in range(2) for s in range(2))]
     return blend((0, 1), units, far, panel, distant, None, total)
 
 

time: 165 us -> 181 us (1.097); the launches traced: 164 us -> 178 us
  starting transfers between devices: 33.6 us -> 60.6 us
  waiting for transfers between devices: 55.1 us -> 47.8 us
  local copies, waits for them, and re-layouts: 13.9 us -> 8.08 us
  Pallas kernels: 46.5 us -> 44.3 us
  between operations: 13.5 us -> 15.5 us
    ppermute x16 -> x15, starting transfers between devices: 33.6 us -> 60.6 us  [move(): return lax.ppermute(array, AXES, pairs)]
    ppermute x16 -> x15, waiting for transfers between devices: 55.1 us -> 47.8 us  [move(): return lax.ppermute(array, AXES, pairs)]
    slice x4 -> x2, local copies, waits for them, and re-layouts: 9.08 us -> 3.57 us  [the longest x1 2.27 us: shards(): ahead[:2]]
    pallas_call x3, Pallas kernels: 46.5 us -> 44.3 us  [blend(): pl.pallas_call(functools.partial(blend_kernel, streams, pieces, fresh is...]
  transfers between devices with their start and end apart: 17 -> 16, of which waited for: 5 -> 6; matrix products, arithmetic and copies ran while one was open for 8% -> 4% of each run, Pallas kernels for 21% -> 18%
where the time goes in v1:
time: 181 us; the launch traced here: 178 us
  starting transfers between devices  60.6 us (33%)
  waiting for transfers between devices  47.8 us (26%)
  Pallas kernels  44.3 us (24%)
  between operations  15.5 us (9%)
  local copies, waits for them, and re-layouts  8.08 us (4%)
  other arithmetic  1.83 us (1%)
    ppermute x15, starting transfers between devices, move(): return lax.ppermute(array, AXES, pairs)  60.6 us
    ppermute x15, waiting for transfers between devices, move(): return lax.ppermute(array, AXES, pairs)  47.8 us
    pallas_call x3, Pallas kernels, blend(): pl.pallas_call(functools.partial(blend_kernel, streams, pieces, fresh is...  44.3 us
  transfers between devices with their start and end apart: 16, of which 6 were waited for; matrix products, arithmetic and copies ran while one was open for 4% of the time, Pallas kernels for 18%

profile of v1, /device:TPU:25, one launch (start us, length us, event | category | flops | bytes accessed | tf_op | source)
XLA Modules:
  0.0 178.1 jit_solution(17842377255400668682)
XLA Ops:
  6.5 0.0 copy-start.1
  6.5 0.0 all-gather.3.cloned.1.call-start
  6.5 1.2 slice.12
  7.7 6.2 %collective-permute-start = (bf16[512,512]{1,0:T(8,128)(2,1)S(1)}, bf16[512,512]{1,0:T(8,128)(2,1)S(1)}, u32[]{:S(2)}, u32[]{:S(2)}) collective-permute-start(bf16[512,512]{1,0:T(8,128)(2,1)S(1)} %slice.12), channel_id=1, source_target_pairs={{0,64},{1,88},{2,32},{3,56},{4,0},{5,24},{6,96},{7,120},{8,72},{9,... | collective-permute-start | bytes 1572872 | tf_op jit(solution)/shard_map/ppermute | solution.py:206
  13.9 8.0 %collective-permute-done = bf16[512,512]{1,0:T(8,128)(2,1)S(1)} collective-permute-done((bf16[512,512]{1,0:T(8,128)(2,1)S(1)}, bf16[512,512]{1,0:T(8,128)(2,1)S(1)}, u32[]{:S(2)}, u32[]{:S(2)}) %collective-permute-start) | collective-permute-done | bytes 524320 | tf_op jit(solution)/shard_map/ppermute | solution.py:206
  21.9 0.0 all-gather.3.cloned.1.call-update
  21.9 0.1 collective-permute-start.3
  22.0 1.2 collective-permute-start.2
  23.3 0.3 collective-permute-start.1
  23.6 0.0 copy-done.1
  23.6 20.9 %collective-permute-start.6 = (bf16[512,512]{1,0:T(8,128)(2,1)S(1)}, bf16[512,512]{1,0:T(8,128)(2,1)S(1)}, u32[]{:S(2)}, u32[]{:S(2)}) collective-permute-start(bf16[512,512]{1,0:T(8,128)(2,1)S(1)} %slice.13), channel_id=1, source_target_pairs={{0,64},{1,88},{2,32},{3,56},{4,0},{5,24},{6,96},{7,120},{8,72},{9,... | collective-permute-start | bytes 1572872 | tf_op jit(solution)/shard_map/ppermute | solution.py:206
  44.5 0.0 collective-permute-done.3
  44.5 0.0 collective-permute-done.2
  44.5 0.0 collective-permute-done.1
  44.6 1.6 pad_maximum_fusion.refs_0_
  46.1 0.0 collective-permute-start.4
  46.1 16.1 %collective-permute-done.6 = bf16[512,512]{1,0:T(8,128)(2,1)S(1)} collective-permute-done((bf16[512,512]{1,0:T(8,128)(2,1)S(1)}, bf16[512,512]{1,0:T(8,128)(2,1)S(1)}, u32[]{:S(2)}, u32[]{:S(2)}) %collective-permute-start.6) | collective-permute-done | bytes 524320 | tf_op jit(solution)/shard_map/ppermute | solution.py:206
  62.2 0.0 collective-permute-start.9
  62.2 0.0 collective-permute-start.8
  62.2 1.5 collective-permute-start.7
  63.7 14.5 %collective-permute-start.12 = (bf16[4,512,512]{2,1,0:T(8,128)(2,1)}, bf16[4,512,512]{2,1,0:T(8,128)(2,1)}, u32[]{:S(2)}, u32[]{:S(2)}) collective-permute-start(bf16[4,512,512]{2,1,0:T(8,128)(2,1)} %pad_maximum_fusion.refs_0_), channel_id=1, source_target_pairs={{0,32},{1,9},{2,34},{3,11},{4,36},{5,13},{6,38},{7,15},{8,40},{9,1... | collective-permute-start | bytes 6291464 | tf_op jit(solution)/shard_map/ppermute | solution.py:206
  78.2 0.0 collective-permute-done.9
  78.2 0.0 collective-permute-done.8
  78.2 6.4 %collective-permute-done.7 = bf16[512,512]{1,0:T(8,128)(2,1)S(1)} collective-permute-done((bf16[512,512]{1,0:T(8,128)(2,1)S(1)}, bf16[512,512]{1,0:T(8,128)(2,1)S(1)}, u32[]{:S(2)}, u32[]{:S(2)}) %collective-permute-start.7) | collective-permute-done | bytes 524320 | tf_op jit(solution)/shard_map/ppermute | solution.py:206
  84.6 0.3 pad_maximum_fusion.1.refs_0_
  84.9 0.0 copy-start
  84.9 13.5 %collective-permute-start.11 = (bf16[4,512,512]{2,1,0:T(8,128)(2,1)S(1)}, bf16[4,512,512]{2,1,0:T(8,128)(2,1)}, u32[]{:S(2)}, u32[]{:S(2)}) collective-permute-start(bf16[4,512,512]{2,1,0:T(8,128)(2,1)S(1)} %pad_maximum_fusion.1.refs_0_), channel_id=1, source_target_pairs={{0,32},{1,9},{2,34},{3,11},{4,36},{5,13},{6,38},{7,15},{8,40},{9,1... | collective-permute-start | bytes 6291464 | tf_op jit(solution)/shard_map/ppermute | solution.py:206
  98.4 0.0 collective-permute-start.10
  98.4 0.0 collective-permute-done.4.refs_1_
  98.4 0.0 collective-permute-start.5
  100.4 0.6 stack.193.table
  101.0 0.5 collective-permute-done.12.refs_2_
  101.5 0.0 all-gather.3.cloned.1.call-done
  101.5 16.1 %shard_map.37.refs_5_ = f32[1024,2048]{1,0:T(8,128)} custom-call(s32[27]{0:T(128)} %stack.193.table, bf16[8,1024,512]{2,1,0:T(8,128)(2,1)} %bitcast.45, bf16[4,512,512]{2,1,0:T(8,128)(2,1)} %pad_maximum_fusion.refs_0_, bf16[4,512,512]{2,1,0:T(8,128)(2,1)} %collective-permute-done.4.refs_1_, bf16[4,512,512]{2,1,0:T(8,128)(2,1)} %collective-permute-done.12.refs_2_, ...), custom_call_target="tpu_custom_call" | custom-call | flops 6442450944 | bytes 25165824 | tf_op jit(solution)/shard_map/pallas_call | solution.py:181
  117.6 0.0 copy-done
  117.6 6.3 %collective-permute-done.11.refs_2_ = bf16[4,512,512]{2,1,0:T(8,128)(2,1)} collective-permute-done((bf16[4,512,512]{2,1,0:T(8,128)(2,1)S(1)}, bf16[4,512,512]{2,1,0:T(8,128)(2,1)}, u32[]{:S(2)}, u32[]{:S(2)}) %collective-permute-start.11) | collective-permute-done | bytes 2097184 | tf_op jit(solution)/shard_map/ppermute | solution.py:206
  123.9 0.0 collective-permute-done.10.refs_1_
  123.9 1.3 slice.15
  125.2 2.3 %slice.14 = bf16[2,512,512]{2,1,0:T(8,128)(2,1)} slice(bf16[4,512,512]{2,1,0:T(8,128)(2,1)} %collective-permute-done.10.refs_1_), slice={[0:2], [0:512], [0:512]} | slice | bytes 2097152 | tf_op jit(solution)/shard_map/slice | solution.py:227
  127.4 1.0 collective-permute-start.13
  128.5 1.3 collective-permute-start.14
  129.8 0.6 stack.157.table
  130.4 16.1 %shard_map.38.refs_3_ = f32[1024,2048]{1,0:T(8,128)} custom-call(s32[27]{0:T(128)} %stack.193.table, bf16[8,1024,512]{2,1,0:T(8,128)(2,1)} %bitcast.46, bf16[4,512,512]{2,1,0:T(8,128)(2,1)} %copy-done, bf16[4,512,512]{2,1,0:T(8,128)(2,1)} %collective-permute-done.10.refs_1_, ...), custom_call_target="tpu_custom_call", output_to_operand_aliasing={{}: (7, {})} | custom-call | flops 6442450944 | bytes 25165824 | tf_op jit(solution)/shard_map/pallas_call | solution.py:181
  146.5 0.0 collective-permute-done.5.refs_0_
  146.5 10.5 %collective-permute-done.13.refs_1_ = bf16[2,512,512]{2,1,0:T(8,128)(2,1)S(1)} collective-permute-done((bf16[2,512,512]{2,1,0:T(8,128)(2,1)}, bf16[2,512,512]{2,1,0:T(8,128)(2,1)S(1)}, u32[]{:S(2)}, u32[]{:S(2)}) %collective-permute-start.13) | collective-permute-done | bytes 1048608 | tf_op jit(solution)/shard_map/ppermute | solution.py:206
  157.0 0.0 copy-start.2
  157.0 0.0 collective-permute-done.14.refs_2_
  157.0 1.1 copy-done.2
  158.1 0.0 copy-start.3
  158.1 1.0 copy-done.3
  159.1 12.2 %shard_map.39 = f32[1024,2048]{1,0:T(8,128)} custom-call(s32[11]{0:T(128)} %stack.157.table, bf16[8,1024,512]{2,1,0:T(8,128)(2,1)} %bitcast.47, bf16[4,512,512]{2,1,0:T(8,128)(2,1)} %collective-permute-done.5.refs_0_, bf16[2,512,512]{2,1,0:T(8,128)(2,1)} %copy-done.2, bf16[2,512,512]{2,1,0:T(8,128)(2,1)} %copy-done.3, ...), custom_call_target="tpu_custom_call", output_to_operand_aliasing={{}: (5, {})} | custom-call | flops 4294967296 | bytes 25165824 | tf_op jit(solution)/shard_map/pallas_call | solution.py:181
  (1 shorter events, 0.0 us)
Async XLA Ops:
  6.5 17.0 %copy-start.1 = (bf16[1024,512]{1,0:T(8,128)(2,1)S(1)}, bf16[1024,512]{1,0:T(8,128)(2,1)}, u32[]{:S(2)}) copy-start(bf16[1024,512]{1,0:T(8,128)(2,1)} %param.5) | copy-start | bytes 3145732
  6.5 95.0 %all-gather.3.cloned.1.call-start = ((), (), s32[]{:S(2)}) async-start(), calls=%async_computation | async-start | bytes 9437184 | tf_op jit(solution)/shard_map/all_gather | solution.py:213
  7.7 14.2 %collective-permute-start = (bf16[512,512]{1,0:T(8,128)(2,1)S(1)}, bf16[512,512]{1,0:T(8,128)(2,1)S(1)}, u32[]{:S(2)}, u32[]{:S(2)}) collective-permute-start(bf16[512,512]{1,0:T(8,128)(2,1)S(1)} %slice.12), channel_id=1, source_target_pairs={{0,64},{1,88},{2,32},{3,56},{4,0},{5,24},{6,96},{7,120},{8,72},{9,... | collective-permute-start | bytes 1572872 | tf_op jit(solution)/shard_map/ppermute | solution.py:206
  21.9 22.6 %collective-permute-start.3 = (bf16[512,512]{1,0:T(8,128)(2,1)S(1)}, bf16[512,512]{1,0:T(8,128)(2,1)S(1)}, u32[]{:S(2)}, u32[]{:S(2)}) collective-permute-start(bf16[512,512]{1,0:T(8,128)(2,1)S(1)} %collective-permute-done), channel_id=1, source_target_pairs={{0,16},{1,65},{2,18},{3,67},{4,20},{5,69},{6,22},{7,71},{8,24},{9,... | collective-permute-start | bytes 1572872 | tf_op jit(solution)/shard_map/ppermute | solution.py:206
  22.0 22.5 %collective-permute-start.2 = (bf16[512,512]{1,0:T(8,128)(2,1)S(1)}, bf16[512,512]{1,0:T(8,128)(2,1)S(1)}, u32[]{:S(2)}, u32[]{:S(2)}) collective-permute-start(bf16[512,512]{1,0:T(8,128)(2,1)S(1)} %collective-permute-done), channel_id=1, source_target_pairs={{0,8},{1,33},{2,10},{3,35},{4,12},{5,37},{6,14},{7,39},{8,16},{9,4... | collective-permute-start | bytes 1572872 | tf_op jit(solution)/shard_map/ppermute | solution.py:206
  23.3 21.3 %collective-permute-start.1 = (bf16[512,512]{1,0:T(8,128)(2,1)S(1)}, bf16[512,512]{1,0:T(8,128)(2,1)S(1)}, u32[]{:S(2)}, u32[]{:S(2)}) collective-permute-start(bf16[512,512]{1,0:T(8,128)(2,1)S(1)} %collective-permute-done), channel_id=1, source_target_pairs={{0,24},{1,97},{2,26},{3,99},{4,28},{5,101},{6,30},{7,103},{8,0},{9... | collective-permute-start | bytes 1572872 | tf_op jit(solution)/shard_map/ppermute | solution.py:206
  23.6 38.6 %collective-permute-start.6 = (bf16[512,512]{1,0:T(8,128)(2,1)S(1)}, bf16[512,512]{1,0:T(8,128)(2,1)S(1)}, u32[]{:S(2)}, u32[]{:S(2)}) collective-permute-start(bf16[512,512]{1,0:T(8,128)(2,1)S(1)} %slice.13), channel_id=1, source_target_pairs={{0,64},{1,88},{2,32},{3,56},{4,0},{5,24},{6,96},{7,120},{8,72},{9,... | collective-permute-start | bytes 1572872 | tf_op jit(solution)/shard_map/ppermute | solution.py:206
  46.1 52.3 %collective-permute-start.4 = (bf16[4,512,512]{2,1,0:T(8,128)(2,1)}, bf16[4,512,512]{2,1,0:T(8,128)(2,1)}, u32[]{:S(2)}, u32[]{:S(2)}) collective-permute-start(bf16[4,512,512]{2,1,0:T(8,128)(2,1)} %pad_maximum_fusion.refs_0_), channel_id=1, source_target_pairs={{0,96},{1,25},{2,98},{3,27},{4,100},{5,29},{6,102},{7,31},{8,104},... | collective-permute-start | bytes 6291464 | tf_op jit(solution)/shard_map/ppermute | solution.py:206
  62.2 16.0 %collective-permute-start.9 = (bf16[512,512]{1,0:T(8,128)(2,1)S(1)}, bf16[512,512]{1,0:T(8,128)(2,1)S(1)}, u32[]{:S(2)}, u32[]{:S(2)}) collective-permute-start(bf16[512,512]{1,0:T(8,128)(2,1)S(1)} %collective-permute-done.6), channel_id=1, source_target_pairs={{0,16},{1,65},{2,18},{3,67},{4,20},{5,69},{6,22},{7,71},{8,24},{9,... | collective-permute-start | bytes 1572872 | tf_op jit(solution)/shard_map/ppermute | solution.py:206
  62.2 16.0 %collective-permute-start.8 = (bf16[512,512]{1,0:T(8,128)(2,1)S(1)}, bf16[512,512]{1,0:T(8,128)(2,1)S(1)}, u32[]{:S(2)}, u32[]{:S(2)}) collective-permute-start(bf16[512,512]{1,0:T(8,128)(2,1)S(1)} %collective-permute-done.6), channel_id=1, source_target_pairs={{0,8},{1,33},{2,10},{3,35},{4,12},{5,37},{6,14},{7,39},{8,16},{9,4... | collective-permute-start | bytes 1572872 | tf_op jit(solution)/shard_map/ppermute | solution.py:206
  62.2 22.4 %collective-permute-start.7 = (bf16[512,512]{1,0:T(8,128)(2,1)S(1)}, bf16[512,512]{1,0:T(8,128)(2,1)S(1)}, u32[]{:S(2)}, u32[]{:S(2)}) collective-permute-start(bf16[512,512]{1,0:T(8,128)(2,1)S(1)} %collective-permute-done.6), channel_id=1, source_target_pairs={{0,24},{1,97},{2,26},{3,99},{4,28},{5,101},{6,30},{7,103},{8,0},{9... | collective-permute-start | bytes 1572872 | tf_op jit(solution)/shard_map/ppermute | solution.py:206
  63.7 37.8 %collective-permute-start.12 = (bf16[4,512,512]{2,1,0:T(8,128)(2,1)}, bf16[4,512,512]{2,1,0:T(8,128)(2,1)}, u32[]{:S(2)}, u32[]{:S(2)}) collective-permute-start(bf16[4,512,512]{2,1,0:T(8,128)(2,1)} %pad_maximum_fusion.refs_0_), channel_id=1, source_target_pairs={{0,32},{1,9},{2,34},{3,11},{4,36},{5,13},{6,38},{7,15},{8,40},{9,1... | collective-permute-start | bytes 6291464 | tf_op jit(solution)/shard_map/ppermute | solution.py:206
  84.9 32.7 %copy-start = (bf16[4,512,512]{2,1,0:T(8,128)(2,1)}, bf16[4,512,512]{2,1,0:T(8,128)(2,1)S(1)}, u32[]{:S(2)}) copy-start(bf16[4,512,512]{2,1,0:T(8,128)(2,1)S(1)} %pad_maximum_fusion.1.refs_0_) | copy-start | bytes 6291460
  84.9 39.0 %collective-permute-start.11 = (bf16[4,512,512]{2,1,0:T(8,128)(2,1)S(1)}, bf16[4,512,512]{2,1,0:T(8,128)(2,1)}, u32[]{:S(2)}, u32[]{:S(2)}) collective-permute-start(bf16[4,512,512]{2,1,0:T(8,128)(2,1)S(1)} %pad_maximum_fusion.1.refs_0_), channel_id=1, source_target_pairs={{0,32},{1,9},{2,34},{3,11},{4,36},{5,13},{6,38},{7,15},{8,40},{9,1... | collective-permute-start | bytes 6291464 | tf_op jit(solution)/shard_map/ppermute | solution.py:206
  98.4 25.5 %collective-permute-start.10 = (bf16[4,512,512]{2,1,0:T(8,128)(2,1)S(1)}, bf16[4,512,512]{2,1,0:T(8,128)(2,1)}, u32[]{:S(2)}, u32[]{:S(2)}) collective-permute-start(bf16[4,512,512]{2,1,0:T(8,128)(2,1)S(1)} %pad_maximum_fusion.1.refs_0_), channel_id=1, source_target_pairs={{0,96},{1,25},{2,98},{3,27},{4,100},{5,29},{6,102},{7,31},{8,104},... | collective-permute-start | bytes 6291464 | tf_op jit(solution)/shard_map/ppermute | solution.py:206
  98.4 48.0 %collective-permute-start.5 = (bf16[4,512,512]{2,1,0:T(8,128)(2,1)}, bf16[4,512,512]{2,1,0:T(8,128)(2,1)}, u32[]{:S(2)}, u32[]{:S(2)}) collective-permute-start(bf16[4,512,512]{2,1,0:T(8,128)(2,1)} %collective-permute-done.4.refs_1_), channel_id=1, source_target_pairs={{0,96},{1,25},{2,98},{3,27},{4,100},{5,29},{6,102},{7,31},{8,104},... | collective-permute-start | bytes 6291464 | tf_op jit(solution)/shard_map/ppermute | solution.py:206
  127.4 29.6 %collective-permute-start.13 = (bf16[2,512,512]{2,1,0:T(8,128)(2,1)}, bf16[2,512,512]{2,1,0:T(8,128)(2,1)S(1)}, u32[]{:S(2)}, u32[]{:S(2)}) collective-permute-start(bf16[2,512,512]{2,1,0:T(8,128)(2,1)} %slice.14), channel_id=1, source_target_pairs={{0,96},{1,25},{2,98},{3,27},{4,100},{5,29},{6,102},{7,31},{8,104},... | collective-permute-start | bytes 3145736 | tf_op jit(solution)/shard_map/ppermute | solution.py:206
  128.5 28.5 %collective-permute-start.14 = (bf16[2,512,512]{2,1,0:T(8,128)(2,1)S(1)}, bf16[2,512,512]{2,1,0:T(8,128)(2,1)S(1)}, u32[]{:S(2)}, u32[]{:S(2)}) collective-permute-start(bf16[2,512,512]{2,1,0:T(8,128)(2,1)S(1)} %slice.15), channel_id=1, source_target_pairs={{0,32},{1,9},{2,34},{3,11},{4,36},{5,13},{6,38},{7,15},{8,40},{9,1... | collective-permute-start | bytes 3145736 | tf_op jit(solution)/shard_map/ppermute | solution.py:206
  157.0 1.1 copy-start.2
  158.1 1.0 copy-start.3
Sparse Core Ops, SparseCore 0:
  22.1 69.4 all-gather.2

commit v2 on v1

--- a/solution.py
+++ b/solution.py
@@ -219,14 +219,17 @@
         own = jnp.stack([unit] + [move(unit, shift_pairs(i, True)) for i in (1, -1, 2)])
         return own, move(own, shift_pairs(1, False)), move(own, shift_pairs(-1, False))
 
+    def forward(ahead, behind):
+        return move(ahead[:2], shift_pairs(1, False)), move(behind[2:], shift_pairs(-1, False))
+
     held = [gather(unit) for unit in heads]
     units = [tuple((g, s) for g in range(3) for s in range(SIDE))]
-    distant = [move(held[0][1], shift_pairs(1, False))]
+    distant = forward(*held[0][1:])
     total = blend((0,), units, near, panel, held[0], inputs, None)
     (own, ahead, behind), total = lax.optimization_barrier((held[1], total))
-    distant += [move(ahead[:2], shift_pairs(1, False)), move(behind[2:], shift_pairs(-1, False))]
+    distant += forward(ahead, behind)
     total = blend((1,), units, near, panel, (own, ahead, behind), inputs, total)
-    units = [tuple((0, s) for s in range(SIDE)), tuple((1 + g, s) for g in range(2) for s in range(2))]
+    units = [tuple((2 * q + g, s) for g in range(2) for s in range(2)) for q in range(STREAMS)]
     return blend((0, 1), units, far, panel, distant, None, total)
 
 

time: 181 us -> 163 us (0.901)
  starting transfers between devices: 60.6 us -> 33.6 us
  waiting for transfers between devices: 47.8 us -> 55.1 us
  local copies, waits for them, and re-layouts: 8.08 us -> 13.9 us
  between operations: 15.5 us -> 13.5 us
    ppermute x15 -> x16, starting transfers between devices: 60.6 us -> 33.6 us  [move(): return lax.ppermute(array, AXES, pairs)]
    ppermute x15 -> x16, waiting for transfers between devices: 47.8 us -> 55.1 us  [move(): return lax.ppermute(array, AXES, pairs)]
    slice x2 -> x4, local copies, waits for them, and re-layouts: 3.57 us -> 9.08 us  [the longest x2 4.55 us: forward(): behind[2:]]
  transfers between devices with their start and end apart: 16 -> 17, of which waited for: 6 -> 5; matrix products, arithmetic and copies ran while one was open for 4% -> 8% of each run, Pallas kernels for 18% -> 20%
where the time goes in v2:
time: 163 us; the launch traced here: 162 us
  waiting for transfers between devices  55.1 us (34%)
  Pallas kernels  44 us (27%)
  starting transfers between devices  33.6 us (21%)
  local copies, waits for them, and re-layouts  13.9 us (9%)
  between operations  13.5 us (8%)
  other arithmetic  1.85 us (1%)
    ppermute x16, waiting for transfers between devices, move(): return lax.ppermute(array, AXES, pairs)  55.1 us
    pallas_call x3, Pallas kernels, blend(): pl.pallas_call(functools.partial(blend_kernel, streams, pieces, fresh is...  44 us
    ppermute x16, starting transfers between devices, move(): return lax.ppermute(array, AXES, pairs)  33.6 us
    slice x2, local copies, waits for them, and re-layouts, forward(): behind[2:]  4.55 us
    slice x2, local copies, waits for them, and re-layouts, forward(): ahead[:2]  4.53 us
  transfers between devices with their start and end apart: 17, of which 5 were waited for; matrix products, arithmetic and copies ran while one was open for 8% of the time, Pallas kernels for 20%

profile of v2, /device:TPU:25, one launch (start us, length us, event | category | flops | bytes accessed | tf_op | source)
XLA Modules:
  0.0 161.9 jit_solution(1554728340771030353)
XLA Ops:
  6.5 0.0 copy-start.1
  6.5 0.0 all-gather.3.cloned.1.call-start
  6.5 1.2 slice.18
  7.7 6.2 %collective-permute-start = (bf16[512,512]{1,0:T(8,128)(2,1)S(1)}, bf16[512,512]{1,0:T(8,128)(2,1)S(1)}, u32[]{:S(2)}, u32[]{:S(2)}) collective-permute-start(bf16[512,512]{1,0:T(8,128)(2,1)S(1)} %slice.18), channel_id=1, source_target_pairs={{0,64},{1,88},{2,32},{3,56},{4,0},{5,24},{6,96},{7,120},{8,72},{9,... | collective-permute-start | bytes 1572872 | tf_op jit(solution)/shard_map/ppermute | solution.py:206
  13.9 8.0 %collective-permute-done = bf16[512,512]{1,0:T(8,128)(2,1)S(1)} collective-permute-done((bf16[512,512]{1,0:T(8,128)(2,1)S(1)}, bf16[512,512]{1,0:T(8,128)(2,1)S(1)}, u32[]{:S(2)}, u32[]{:S(2)}) %collective-permute-start) | collective-permute-done | bytes 524320 | tf_op jit(solution)/shard_map/ppermute | solution.py:206
  21.9 0.0 all-gather.3.cloned.1.call-update
  21.9 0.0 copy-done.1
  22.0 6.2 %collective-permute-start.8 = (bf16[512,512]{1,0:T(8,128)(2,1)S(1)}, bf16[512,512]{1,0:T(8,128)(2,1)S(1)}, u32[]{:S(2)}, u32[]{:S(2)}) collective-permute-start(bf16[512,512]{1,0:T(8,128)(2,1)S(1)} %slice.21), channel_id=1, source_target_pairs={{0,64},{1,88},{2,32},{3,56},{4,0},{5,24},{6,96},{7,120},{8,72},{9,... | collective-permute-start | bytes 1572872 | tf_op jit(solution)/shard_map/ppermute | solution.py:206
  28.2 0.0 collective-permute-start.3
  28.2 1.2 collective-permute-start.2
  29.4 0.2 collective-permute-start.1
  29.7 13.6 %collective-permute-done.8 = bf16[512,512]{1,0:T(8,128)(2,1)S(1)} collective-permute-done((bf16[512,512]{1,0:T(8,128)(2,1)S(1)}, bf16[512,512]{1,0:T(8,128)(2,1)S(1)}, u32[]{:S(2)}, u32[]{:S(2)}) %collective-permute-start.8) | collective-permute-done | bytes 524320 | tf_op jit(solution)/shard_map/ppermute | solution.py:206
  43.3 0.0 collective-permute-start.11
  43.3 0.1 collective-permute-start.10
  43.4 0.0 collective-permute-done.3
  43.4 1.3 collective-permute-start.9
  44.8 10.5 %collective-permute-done.2 = bf16[512,512]{1,0:T(8,128)(2,1)S(1)} collective-permute-done((bf16[512,512]{1,0:T(8,128)(2,1)S(1)}, bf16[512,512]{1,0:T(8,128)(2,1)S(1)}, u32[]{:S(2)}, u32[]{:S(2)}) %collective-permute-start.2) | collective-permute-done | bytes 524320 | tf_op jit(solution)/shard_map/ppermute | solution.py:206
  55.3 0.0 collective-permute-done.1
  55.3 1.6 pad_maximum_fusion.refs_0_
  56.9 0.0 collective-permute-start.6
  56.9 2.7 %collective-permute-start.4 = (bf16[4,512,512]{2,1,0:T(8,128)(2,1)}, bf16[4,512,512]{2,1,0:T(8,128)(2,1)}, u32[]{:S(2)}, u32[]{:S(2)}) collective-permute-start(bf16[4,512,512]{2,1,0:T(8,128)(2,1)} %pad_maximum_fusion.refs_0_), channel_id=1, source_target_pairs={{0,96},{1,25},{2,98},{3,27},{4,100},{5,29},{6,102},{7,31},{8,104},... | collective-permute-start | bytes 6291464 | tf_op jit(solution)/shard_map/ppermute | solution.py:206
  59.5 0.0 collective-permute-done.11
  59.5 1.4 collective-permute-done.10
  61.0 0.0 collective-permute-done.9
  61.0 0.3 pad_maximum_fusion.1.refs_0_
  61.3 0.0 copy-start
  61.3 0.1 collective-permute-start.13
  61.4 11.3 %collective-permute-start.12 = (bf16[4,512,512]{2,1,0:T(8,128)(2,1)S(1)}, bf16[4,512,512]{2,1,0:T(8,128)(2,1)}, u32[]{:S(2)}, u32[]{:S(2)}) collective-permute-start(bf16[4,512,512]{2,1,0:T(8,128)(2,1)S(1)} %pad_maximum_fusion.1.refs_0_), channel_id=1, source_target_pairs={{0,96},{1,25},{2,98},{3,27},{4,100},{5,29},{6,102},{7,31},{8,104},... | collective-permute-start | bytes 6291464 | tf_op jit(solution)/shard_map/ppermute | solution.py:206
  72.6 0.7 stack.193.table
  73.3 21.5 %collective-permute-done.6.refs_2_ = bf16[4,512,512]{2,1,0:T(8,128)(2,1)} collective-permute-done((bf16[4,512,512]{2,1,0:T(8,128)(2,1)}, bf16[4,512,512]{2,1,0:T(8,128)(2,1)}, u32[]{:S(2)}, u32[]{:S(2)}) %collective-permute-start.6) | collective-permute-done | bytes 2097184 | tf_op jit(solution)/shard_map/ppermute | solution.py:206
  94.8 2.3 %slice.25 = bf16[2,512,512]{2,1,0:T(8,128)(2,1)} slice(bf16[4,512,512]{2,1,0:T(8,128)(2,1)} %collective-permute-done.6.refs_2_), slice={[2:4], [0:512], [0:512]} | slice | bytes 2097152 | tf_op jit(solution)/shard_map/slice | solution.py:223
  97.1 0.0 copy-done
  97.1 0.0 collective-permute-start.7
  97.1 0.0 collective-permute-done.4.refs_1_
  97.1 2.3 %slice.24 = bf16[2,512,512]{2,1,0:T(8,128)(2,1)} slice(bf16[4,512,512]{2,1,0:T(8,128)(2,1)} %collective-permute-done.4.refs_1_), slice={[0:2], [0:512], [0:512]} | slice | bytes 2097152 | tf_op jit(solution)/shard_map/slice | solution.py:223
  99.4 2.7 %collective-permute-start.5 = (bf16[2,512,512]{2,1,0:T(8,128)(2,1)}, bf16[2,512,512]{2,1,0:T(8,128)(2,1)}, u32[]{:S(2)}, u32[]{:S(2)}) collective-permute-start(bf16[2,512,512]{2,1,0:T(8,128)(2,1)} %slice.24), channel_id=1, source_target_pairs={{0,96},{1,25},{2,98},{3,27},{4,100},{5,29},{6,102},{7,31},{8,104},... | collective-permute-start | bytes 3145736 | tf_op jit(solution)/shard_map/ppermute | solution.py:206
  102.0 0.0 all-gather.3.cloned.1.call-done
  102.0 15.9 %shard_map.37.refs_5_ = f32[1024,2048]{1,0:T(8,128)} custom-call(s32[27]{0:T(128)} %stack.193.table, bf16[8,1024,512]{2,1,0:T(8,128)(2,1)} %bitcast.45, bf16[4,512,512]{2,1,0:T(8,128)(2,1)} %pad_maximum_fusion.refs_0_, bf16[4,512,512]{2,1,0:T(8,128)(2,1)} %collective-permute-done.4.refs_1_, bf16[4,512,512]{2,1,0:T(8,128)(2,1)} %collective-permute-done.6.refs_2_, ...), custom_call_target="tpu_custom_call" | custom-call | flops 6442450944 | bytes 25165824 | tf_op jit(solution)/shard_map/pallas_call | solution.py:181
  117.9 0.0 collective-permute-done.13.refs_2_
  118.0 0.0 collective-permute-done.12.refs_1_
  118.0 2.3 %slice.23 = bf16[2,512,512]{2,1,0:T(8,128)(2,1)} slice(bf16[4,512,512]{2,1,0:T(8,128)(2,1)} %collective-permute-done.13.refs_2_), slice={[2:4], [0:512], [0:512]} | slice | bytes 2097152 | tf_op jit(solution)/shard_map/slice | solution.py:223
  120.3 2.3 %slice.22 = bf16[2,512,512]{2,1,0:T(8,128)(2,1)} slice(bf16[4,512,512]{2,1,0:T(8,128)(2,1)} %collective-permute-done.12.refs_1_), slice={[0:2], [0:512], [0:512]} | slice | bytes 2097152 | tf_op jit(solution)/shard_map/slice | solution.py:223
  122.5 1.0 collective-permute-start.14
  123.5 0.5 collective-permute-start.15
  124.0 0.7 stack.157.table
  124.7 15.9 %shard_map.38.refs_4_ = f32[1024,2048]{1,0:T(8,128)} custom-call(s32[27]{0:T(128)} %stack.193.table, bf16[8,1024,512]{2,1,0:T(8,128)(2,1)} %bitcast.46, bf16[4,512,512]{2,1,0:T(8,128)(2,1)} %copy-done, bf16[4,512,512]{2,1,0:T(8,128)(2,1)} %collective-permute-done.12.refs_1_, ...), custom_call_target="tpu_custom_call", output_to_operand_aliasing={{}: (7, {})} | custom-call | flops 6442450944 | bytes 25165824 | tf_op jit(solution)/shard_map/pallas_call | solution.py:181
  140.6 0.0 collective-permute-done.7.refs_1_
  140.6 0.0 copy-start.2
  140.6 0.0 collective-permute-done.5.refs_0_
  140.6 0.0 collective-permute-done.14.refs_2_
  140.6 0.0 copy-start.3
  140.6 0.0 collective-permute-done.15.refs_3_
  140.6 0.9 copy-done.2
  141.6 0.3 copy-done.3
  141.9 0.0 copy-start.4
  141.9 1.0 copy-done.4
  142.9 12.2 %shard_map.39 = f32[1024,2048]{1,0:T(8,128)} custom-call(s32[11]{0:T(128)} %stack.157.table, bf16[8,1024,512]{2,1,0:T(8,128)(2,1)} %bitcast.47, bf16[2,512,512]{2,1,0:T(8,128)(2,1)} %collective-permute-done.5.refs_0_, bf16[2,512,512]{2,1,0:T(8,128)(2,1)} %copy-done.2, bf16[2,512,512]{2,1,0:T(8,128)(2,1)} %copy-done.3, ...), custom_call_target="tpu_custom_call", output_to_operand_aliasing={{}: (6, {})} | custom-call | flops 4294967296 | bytes 25165824 | tf_op jit(solution)/shard_map/pallas_call | solution.py:181
  (1 shorter events, 0.0 us)
Async XLA Ops:
  6.5 15.4 %copy-start.1 = (bf16[1024,512]{1,0:T(8,128)(2,1)S(1)}, bf16[1024,512]{1,0:T(8,128)(2,1)}, u32[]{:S(2)}) copy-start(bf16[1024,512]{1,0:T(8,128)(2,1)} %param.5) | copy-start | bytes 3145732
  6.5 95.5 %all-gather.3.cloned.1.call-start = ((), (), s32[]{:S(2)}) async-start(), calls=%async_computation | async-start | bytes 9437184 | tf_op jit(solution)/shard_map/all_gather | solution.py:213
  7.7 14.2 %collective-permute-start = (bf16[512,512]{1,0:T(8,128)(2,1)S(1)}, bf16[512,512]{1,0:T(8,128)(2,1)S(1)}, u32[]{:S(2)}, u32[]{:S(2)}) collective-permute-start(bf16[512,512]{1,0:T(8,128)(2,1)S(1)} %slice.18), channel_id=1, source_target_pairs={{0,64},{1,88},{2,32},{3,56},{4,0},{5,24},{6,96},{7,120},{8,72},{9,... | collective-permute-start | bytes 1572872 | tf_op jit(solution)/shard_map/ppermute | solution.py:206
  22.0 21.3 %collective-permute-start.8 = (bf16[512,512]{1,0:T(8,128)(2,1)S(1)}, bf16[512,512]{1,0:T(8,128)(2,1)S(1)}, u32[]{:S(2)}, u32[]{:S(2)}) collective-permute-start(bf16[512,512]{1,0:T(8,128)(2,1)S(1)} %slice.21), channel_id=1, source_target_pairs={{0,64},{1,88},{2,32},{3,56},{4,0},{5,24},{6,96},{7,120},{8,72},{9,... | collective-permute-start | bytes 1572872 | tf_op jit(solution)/shard_map/ppermute | solution.py:206
  28.2 15.2 %collective-permute-start.3 = (bf16[512,512]{1,0:T(8,128)(2,1)S(1)}, bf16[512,512]{1,0:T(8,128)(2,1)S(1)}, u32[]{:S(2)}, u32[]{:S(2)}) collective-permute-start(bf16[512,512]{1,0:T(8,128)(2,1)S(1)} %collective-permute-done), channel_id=1, source_target_pairs={{0,16},{1,65},{2,18},{3,67},{4,20},{5,69},{6,22},{7,71},{8,24},{9,... | collective-permute-start | bytes 1572872 | tf_op jit(solution)/shard_map/ppermute | solution.py:206
  28.2 27.0 %collective-permute-start.2 = (bf16[512,512]{1,0:T(8,128)(2,1)S(1)}, bf16[512,512]{1,0:T(8,128)(2,1)S(1)}, u32[]{:S(2)}, u32[]{:S(2)}) collective-permute-start(bf16[512,512]{1,0:T(8,128)(2,1)S(1)} %collective-permute-done), channel_id=1, source_target_pairs={{0,8},{1,33},{2,10},{3,35},{4,12},{5,37},{6,14},{7,39},{8,16},{9,4... | collective-permute-start | bytes 1572872 | tf_op jit(solution)/shard_map/ppermute | solution.py:206
  29.4 25.8 %collective-permute-start.1 = (bf16[512,512]{1,0:T(8,128)(2,1)S(1)}, bf16[512,512]{1,0:T(8,128)(2,1)S(1)}, u32[]{:S(2)}, u32[]{:S(2)}) collective-permute-start(bf16[512,512]{1,0:T(8,128)(2,1)S(1)} %collective-permute-done), channel_id=1, source_target_pairs={{0,24},{1,97},{2,26},{3,99},{4,28},{5,101},{6,30},{7,103},{8,0},{9... | collective-permute-start | bytes 1572872 | tf_op jit(solution)/shard_map/ppermute | solution.py:206
  43.3 16.2 %collective-permute-start.11 = (bf16[512,512]{1,0:T(8,128)(2,1)S(1)}, bf16[512,512]{1,0:T(8,128)(2,1)S(1)}, u32[]{:S(2)}, u32[]{:S(2)}) collective-permute-start(bf16[512,512]{1,0:T(8,128)(2,1)S(1)} %collective-permute-done.8), channel_id=1, source_target_pairs={{0,16},{1,65},{2,18},{3,67},{4,20},{5,69},{6,22},{7,71},{8,24},{9,... | collective-permute-start | bytes 1572872 | tf_op jit(solution)/shard_map/ppermute | solution.py:206
  43.3 17.7 %collective-permute-start.10 = (bf16[512,512]{1,0:T(8,128)(2,1)S(1)}, bf16[512,512]{1,0:T(8,128)(2,1)S(1)}, u32[]{:S(2)}, u32[]{:S(2)}) collective-permute-start(bf16[512,512]{1,0:T(8,128)(2,1)S(1)} %collective-permute-done.8), channel_id=1, source_target_pairs={{0,8},{1,33},{2,10},{3,35},{4,12},{5,37},{6,14},{7,39},{8,16},{9,4... | collective-permute-start | bytes 1572872 | tf_op jit(solution)/shard_map/ppermute | solution.py:206
  43.4 17.6 %collective-permute-start.9 = (bf16[512,512]{1,0:T(8,128)(2,1)S(1)}, bf16[512,512]{1,0:T(8,128)(2,1)S(1)}, u32[]{:S(2)}, u32[]{:S(2)}) collective-permute-start(bf16[512,512]{1,0:T(8,128)(2,1)S(1)} %collective-permute-done.8), channel_id=1, source_target_pairs={{0,24},{1,97},{2,26},{3,99},{4,28},{5,101},{6,30},{7,103},{8,0},{9... | collective-permute-start | bytes 1572872 | tf_op jit(solution)/shard_map/ppermute | solution.py:206
  56.9 37.9 %collective-permute-start.6 = (bf16[4,512,512]{2,1,0:T(8,128)(2,1)}, bf16[4,512,512]{2,1,0:T(8,128)(2,1)}, u32[]{:S(2)}, u32[]{:S(2)}) collective-permute-start(bf16[4,512,512]{2,1,0:T(8,128)(2,1)} %pad_maximum_fusion.refs_0_), channel_id=1, source_target_pairs={{0,32},{1,9},{2,34},{3,11},{4,36},{5,13},{6,38},{7,15},{8,40},{9,1... | collective-permute-start | bytes 6291464 | tf_op jit(solution)/shard_map/ppermute | solution.py:206
  56.9 40.2 %collective-permute-start.4 = (bf16[4,512,512]{2,1,0:T(8,128)(2,1)}, bf16[4,512,512]{2,1,0:T(8,128)(2,1)}, u32[]{:S(2)}, u32[]{:S(2)}) collective-permute-start(bf16[4,512,512]{2,1,0:T(8,128)(2,1)} %pad_maximum_fusion.refs_0_), channel_id=1, source_target_pairs={{0,96},{1,25},{2,98},{3,27},{4,100},{5,29},{6,102},{7,31},{8,104},... | collective-permute-start | bytes 6291464 | tf_op jit(solution)/shard_map/ppermute | solution.py:206
  61.3 35.8 %copy-start = (bf16[4,512,512]{2,1,0:T(8,128)(2,1)}, bf16[4,512,512]{2,1,0:T(8,128)(2,1)S(1)}, u32[]{:S(2)}) copy-start(bf16[4,512,512]{2,1,0:T(8,128)(2,1)S(1)} %pad_maximum_fusion.1.refs_0_) | copy-start | bytes 6291460
  61.3 56.7 %collective-permute-start.13 = (bf16[4,512,512]{2,1,0:T(8,128)(2,1)S(1)}, bf16[4,512,512]{2,1,0:T(8,128)(2,1)}, u32[]{:S(2)}, u32[]{:S(2)}) collective-permute-start(bf16[4,512,512]{2,1,0:T(8,128)(2,1)S(1)} %pad_maximum_fusion.1.refs_0_), channel_id=1, source_target_pairs={{0,32},{1,9},{2,34},{3,11},{4,36},{5,13},{6,38},{7,15},{8,40},{9,1... | collective-permute-start | bytes 6291464 | tf_op jit(solution)/shard_map/ppermute | solution.py:206
  61.4 56.6 %collective-permute-start.12 = (bf16[4,512,512]{2,1,0:T(8,128)(2,1)S(1)}, bf16[4,512,512]{2,1,0:T(8,128)(2,1)}, u32[]{:S(2)}, u32[]{:S(2)}) collective-permute-start(bf16[4,512,512]{2,1,0:T(8,128)(2,1)S(1)} %pad_maximum_fusion.1.refs_0_), channel_id=1, source_target_pairs={{0,96},{1,25},{2,98},{3,27},{4,100},{5,29},{6,102},{7,31},{8,104},... | collective-permute-start | bytes 6291464 | tf_op jit(solution)/shard_map/ppermute | solution.py:206
  97.1 43.5 %collective-permute-start.7 = (bf16[2,512,512]{2,1,0:T(8,128)(2,1)}, bf16[2,512,512]{2,1,0:T(8,128)(2,1)S(1)}, u32[]{:S(2)}, u32[]{:S(2)}) collective-permute-start(bf16[2,512,512]{2,1,0:T(8,128)(2,1)} %slice.25), channel_id=1, source_target_pairs={{0,32},{1,9},{2,34},{3,11},{4,36},{5,13},{6,38},{7,15},{8,40},{9,1... | collective-permute-start | bytes 3145736 | tf_op jit(solution)/shard_map/ppermute | solution.py:206
  99.4 41.3 %collective-permute-start.5 = (bf16[2,512,512]{2,1,0:T(8,128)(2,1)}, bf16[2,512,512]{2,1,0:T(8,128)(2,1)}, u32[]{:S(2)}, u32[]{:S(2)}) collective-permute-start(bf16[2,512,512]{2,1,0:T(8,128)(2,1)} %slice.24), channel_id=1, source_target_pairs={{0,96},{1,25},{2,98},{3,27},{4,100},{5,29},{6,102},{7,31},{8,104},... | collective-permute-start | bytes 3145736 | tf_op jit(solution)/shard_map/ppermute | solution.py:206
  122.5 18.1 %collective-permute-start.14 = (bf16[2,512,512]{2,1,0:T(8,128)(2,1)}, bf16[2,512,512]{2,1,0:T(8,128)(2,1)S(1)}, u32[]{:S(2)}, u32[]{:S(2)}) collective-permute-start(bf16[2,512,512]{2,1,0:T(8,128)(2,1)} %slice.22), channel_id=1, source_target_pairs={{0,96},{1,25},{2,98},{3,27},{4,100},{5,29},{6,102},{7,31},{8,104},... | collective-permute-start | bytes 3145736 | tf_op jit(solution)/shard_map/ppermute | solution.py:206
  123.5 17.1 %collective-permute-start.15 = (bf16[2,512,512]{2,1,0:T(8,128)(2,1)}, bf16[2,512,512]{2,1,0:T(8,128)(2,1)S(1)}, u32[]{:S(2)}, u32[]{:S(2)}) collective-permute-start(bf16[2,512,512]{2,1,0:T(8,128)(2,1)} %slice.23), channel_id=1, source_target_pairs={{0,32},{1,9},{2,34},{3,11},{4,36},{5,13},{6,38},{7,15},{8,40},{9,1... | collective-permute-start | bytes 3145736 | tf_op jit(solution)/shard_map/ppermute | solution.py:206
  140.6 1.0 copy-start.2
  140.6 1.3 copy-start.3
  141.9 1.0 copy-start.4
Sparse Core Ops, SparseCore 0:
  22.1 65.3 all-gather.2
